TPU v7x, 32 devices: a whole 2x2x4 slice. The times are simulated.
32 devices in a mesh: dp: 2 (over x), expert: 16 (over z, y, core).
Axes of the slice: x: 2, y: 2, z: 4, core: 2. Of those that a mesh axis runs over, the one named last changes fastest.
Arguments:
- tokens: bfloat16 [4096, 1024], P(('dp', 'expert')), may hold values from -6 to 6
- cotangent: bfloat16 [4096, 1024], P(('dp', 'expert')), may hold values from -6 to 6
- pick_lists: int32 [2, 16, 128], P('dp'), may hold values from 0 to 2047, as said below
- combine: float32 [2, 16, 128], P('dp'), may hold values from 0.1 to 1
- w_gate: bfloat16 [16, 1024, 1024], P('expert', 'dp'), may hold values from -0.1875 to 0.1875
- w_up: bfloat16 [16, 1024, 1024], P('expert', 'dp'), may hold values from -0.1875 to 0.1875
- w_down: bfloat16 [16, 1024, 1024], P('expert', 'dp'), may hold values from -0.1875 to 0.1875
Outputs:
- layer_out: bfloat16 [4096, 1024], P(('dp', 'expert'))
- tokens_grad: bfloat16 [4096, 1024], P(('dp', 'expert'))
- grad_gate: bfloat16 [16, 1024, 1024], P('expert', 'dp')
- grad_up: bfloat16 [16, 1024, 1024], P('expert', 'dp')
- grad_down: bfloat16 [16, 1024, 1024], P('expert', 'dp')
Inputs may be any that keep to these rules, and one draw needn't show every extreme that they name: Each list pick_lists[r, e] names 128 distinct tokens of replica r. Token numbers j * 128 to (j + 1) * 128 - 1 are those of the device with index j on the expert axis; at most 16 picks of one expert in one replica fall among one device's tokens, and for every expert and replica exactly 16 fall among some device's.
All inputs are finite; a program needn't handle non-finite values.
Results may differ from a plain program's by a relative error of at most 0.013.
Values may be sent and summed in bfloat16 or wider, within the bound.
A program may use at most 64 MiB of HBM per device.

v0:
```python
import jax
import jax.numpy as jnp
from jax import lax
from jax.sharding import PartitionSpec as P


def silu_parts(gate_pre):
    sigma_gate = jax.nn.sigmoid(gate_pre)
    return (gate_pre * sigma_gate, sigma_gate)


def project_hidden(row_block, gate_w, up_w):
    dims = (((1,), (1,)), ((), ()))
    gate_pre = lax.dot_general(row_block, gate_w, dims, preferred_element_type=jnp.float32)
    up_pre = lax.dot_general(row_block, up_w, dims, preferred_element_type=jnp.float32)
    silu_gate, sigma_gate = silu_parts(gate_pre)
    hidden = (silu_gate * up_pre).astype(jnp.bfloat16)
    return (gate_pre, up_pre, silu_gate, sigma_gate, hidden)


def backward_terms(grad_block, gate_pre, up_pre, silu_gate, sigma_gate, gate_w, up_w, down_w):
    dims = (((1,), (1,)), ((), ()))
    d_hidden = lax.dot_general(grad_block, down_w, dims, preferred_element_type=jnp.float32)
    d_gate = (d_hidden * up_pre * sigma_gate * (1.0 + gate_pre * (1.0 - sigma_gate))).astype(
        jnp.bfloat16
    )
    d_up = (d_hidden * silu_gate).astype(jnp.bfloat16)
    back_part = jnp.dot(d_gate, gate_w, preferred_element_type=jnp.float32) + jnp.dot(
        d_up, up_w, preferred_element_type=jnp.float32
    )
    return (d_gate, d_up, back_part)


def weight_grads(row_block, grad_block, hidden, d_gate, d_up):
    dims = (((0,), (0,)), ((), ()))
    grad_gate = lax.dot_general(d_gate, row_block, dims, preferred_element_type=jnp.float32).astype(
        jnp.bfloat16
    )
    grad_up = lax.dot_general(d_up, row_block, dims, preferred_element_type=jnp.float32).astype(
        jnp.bfloat16
    )
    grad_down = lax.dot_general(
        hidden, grad_block, dims, preferred_element_type=jnp.float32
    ).astype(jnp.bfloat16)
    return (grad_gate, grad_up, grad_down)


def per_device(tokens, cotangent, pick_lists, combine, w_gate, w_up, w_down):
    n_experts = lax.axis_size("expert")
    my_index = lax.axis_index("expert")
    tok_rows = tokens.shape[0]
    feat_width = tokens.shape[1]
    capacity = pick_lists.shape[2]
    slot_count = max(2, (2 * capacity + n_experts - 1) // n_experts)
    list_all = pick_lists[0]
    weight_all = combine[0]
    source_dev = list_all // tok_rows
    within_dev = list_all - source_dev * tok_rows
    is_mine = (source_dev == my_index).astype(jnp.int32)
    rank_mine = jnp.cumsum(is_mine, axis=1) - 1
    slot_ids = jnp.arange(slot_count, dtype=jnp.int32)
    select_mask = (is_mine[:, :, None] == 1) & (rank_mine[:, :, None] == slot_ids[None, None, :])
    select_int = select_mask.astype(jnp.int32)
    flat_row = jnp.sum(select_int * within_dev[:, :, None], axis=1).reshape(-1)
    flat_valid = (jnp.sum(select_int, axis=1) > 0).reshape(-1)
    flat_weight = jnp.sum(jnp.where(select_mask, weight_all[:, :, None], 0.0), axis=1).reshape(-1)
    slot_shape = (n_experts, slot_count, feat_width)
    row_send = jnp.where(
        flat_valid[:, None], jnp.take(tokens, flat_row, axis=0), jnp.zeros((), jnp.bfloat16)
    ).reshape(slot_shape)
    cot_rows = jnp.take(cotangent, flat_row, axis=0).astype(jnp.float32)
    grad_send = (
        jnp.where(flat_valid[:, None], flat_weight[:, None] * cot_rows, 0.0)
        .astype(jnp.bfloat16)
        .reshape(slot_shape)
    )
    own_source = lax.dynamic_index_in_dim(source_dev, my_index, 0, keepdims=False)
    order_ids = jnp.arange(capacity, dtype=jnp.int32)
    earlier = order_ids[:, None] > order_ids[None, :]
    same_source = own_source[:, None] == own_source[None, :]
    own_rank = jnp.sum((earlier & same_source).astype(jnp.int32), axis=1)
    position = own_source * slot_count + own_rank

    def compact(received):
        return jnp.take(received.reshape(n_experts * slot_count, feat_width), position, axis=0)

    def expand(result_rows):
        empty_slots = jnp.zeros((n_experts * slot_count, feat_width), jnp.bfloat16)
        return empty_slots.at[position].set(result_rows.astype(jnp.bfloat16)).reshape(slot_shape)

    gate_w = w_gate[0]
    up_w = w_up[0]
    down_w = w_down[0]
    recv_rows = lax.all_to_all(row_send, "expert", split_axis=0, concat_axis=0, tiled=True)
    row_block = lax.all_gather(compact(recv_rows), "dp", axis=0, tiled=True)
    gate_pre, up_pre, silu_gate, sigma_gate, hidden = project_hidden(row_block, gate_w, up_w)
    out_part = jnp.dot(hidden, down_w, preferred_element_type=jnp.float32)
    out_rows = lax.psum_scatter(
        out_part.astype(jnp.bfloat16), "dp", scatter_dimension=0, tiled=True
    ).astype(jnp.float32)
    out_slots = lax.all_to_all(expand(out_rows), "expert", split_axis=0, concat_axis=0, tiled=True)
    recv_grads = lax.all_to_all(grad_send, "expert", split_axis=0, concat_axis=0, tiled=True)
    grad_block = lax.all_gather(compact(recv_grads), "dp", axis=0, tiled=True)
    d_gate, d_up, back_part = backward_terms(
        grad_block, gate_pre, up_pre, silu_gate, sigma_gate, gate_w, up_w, down_w
    )
    back_rows = lax.psum_scatter(
        back_part.astype(jnp.bfloat16), "dp", scatter_dimension=0, tiled=True
    ).astype(jnp.float32)
    back_slots = lax.all_to_all(
        expand(back_rows), "expert", split_axis=0, concat_axis=0, tiled=True
    )
    grad_gate, grad_up, grad_down = weight_grads(row_block, grad_block, hidden, d_gate, d_up)
    out_flat = jnp.where(
        flat_valid[:, None],
        flat_weight[:, None] * out_slots.reshape(-1, feat_width).astype(jnp.float32),
        0.0,
    )
    layer_out = (
        jnp.zeros((tok_rows, feat_width), jnp.float32)
        .at[flat_row]
        .add(out_flat)
        .astype(jnp.bfloat16)
    )
    back_flat = jnp.where(
        flat_valid[:, None], back_slots.reshape(-1, feat_width).astype(jnp.float32), 0.0
    )
    tokens_grad = (
        jnp.zeros((tok_rows, feat_width), jnp.float32)
        .at[flat_row]
        .add(back_flat)
        .astype(jnp.bfloat16)
    )
    return (layer_out, tokens_grad, grad_gate[None], grad_up[None], grad_down[None])


def solution(mesh):
    placed = (
        P(("dp", "expert"), None),
        P(("dp", "expert"), None),
        P("dp", None, None),
        P("dp", None, None),
        P("expert", "dp", None),
        P("expert", "dp", None),
        P("expert", "dp", None),
    )
    return jax.shard_map(
        per_device,
        mesh=mesh,
        in_specs=placed,
        out_specs=(
            P(("dp", "expert"), None),
            P(("dp", "expert"), None),
            P("expert", "dp", None),
            P("expert", "dp", None),
            P("expert", "dp", None),
        ),
        check_vma=False,
    )
```

profile of v0, /device:TPU:0, one launch (start us, length us, event | category | flops | bytes accessed | tf_op | source)
XLA Modules:
  0.0 143.5 jit_solution(17958454077309181270)
XLA Ops:
  10.7 2.5 %gather_fusion.2 = bf16[256,1024]{1,0:T(8,128)(2,1)S(1)} fusion(bf16[128,1024]{1,0:T(8,128)(2,1)} %param.12, s32[1024]{0:T(1024)S(1)} %pad_clamp_fusion.1), kind=kCustom, calls=%fused_computation.2.clone | custom fusion | bytes 1049600 | tf_op jit(solution)/shard_map/jit(_take)/gather | solution.py:71
  14.3 7.4 %all-to-all-start.2 = ((bf16[16,16,1024]{2,1,0:T(8,128)(2,1)}), bf16[16,16,1024]{2,1,0:T(8,128)(2,1)S(1)}, u32[]{:S(2)}, u32[]{:S(2)}) async-start(bf16[16,16,1024]{2,1,0:T(8,128)(2,1)} %bitcast.14), calls=%async_computation.3 | async-start | bytes 1048576 | tf_op jit(solution)/shard_map/all_to_all | solution.py:102
  23.9 12.4 %all-to-all-done.2 = bf16[16,16,1024]{2,1,0:T(8,128)(2,1)S(1)} async-done(((bf16[16,16,1024]{2,1,0:T(8,128)(2,1)}), bf16[16,16,1024]{2,1,0:T(8,128)(2,1)S(1)}, u32[]{:S(2)}, u32[]{:S(2)}) %all-to-all-start.2) | async-done | bytes 524320 | tf_op jit(solution)/shard_map/all_to_all | solution.py:102
  36.2 4.1 %all-to-all-start = ((bf16[16,16,1024]{2,1,0:T(8,128)(2,1)}), bf16[16,16,1024]{2,1,0:T(8,128)(2,1)S(1)}, u32[]{:S(2)}, u32[]{:S(2)}) async-start(bf16[16,16,1024]{2,1,0:T(8,128)(2,1)} %bitcast.7), calls=%async_computation | async-start | bytes 1048576 | tf_op jit(solution)/shard_map/all_to_all | solution.py:94
  41.5 13.3 %all-to-all-done = bf16[16,16,1024]{2,1,0:T(8,128)(2,1)S(1)} async-done(((bf16[16,16,1024]{2,1,0:T(8,128)(2,1)}), bf16[16,16,1024]{2,1,0:T(8,128)(2,1)S(1)}, u32[]{:S(2)}, u32[]{:S(2)}) %all-to-all-start) | async-done | bytes 524320 | tf_op jit(solution)/shard_map/all_to_all | solution.py:94
  55.8 9.0 %all_gather.6 = bf16[256,1024]{1,0:T(8,128)(2,1)S(1)} all-gather(bf16[128,1024]{1,0:T(8,128)(2,1)S(1)} %get-tuple-element.19), channel_id=1, replica_groups=mesh['dp'=2,'expert'=16] {'dp'}, dimensions={0}, use_global_device_ids=true | all-gather | bytes 786432 | tf_op jit(solution)/shard_map/all_gather | solution.py:95
  66.5 8.1 %all_gather.7 = bf16[256,1024]{1,0:T(8,128)(2,1)S(1)} all-gather(bf16[128,1024]{1,0:T(8,128)(2,1)S(1)} %get-tuple-element.18), channel_id=1, replica_groups=mesh['dp'=2,'expert'=16] {'dp'}, dimensions={0}, use_global_device_ids=true | all-gather | bytes 786432 | tf_op jit(solution)/shard_map/all_gather | solution.py:103
  74.6 1.4 multiply_convert_fusion
  76.0 1.2 convolution_convert_fusion.3
  77.3 1.5 %fusion.14 = f32[256,1024]{1,0:T(8,128)S(1)} fusion(bf16[256,512]{1,0:T(8,128)(2,1)} %get-tuple-element.14, bf16[1,512,1024]{2,1,0:T(8,128)(2,1)S(1)} %copy-done.2), kind=kOutput, calls=%fused_computation.28 | convolution fusion | flops 268435456 | bytes 2359296 | tf_op jit(solution)/shard_map/dot_general | solution.py:28
  78.8 1.2 fusion.3
  80.1 11.8 %reduce-scatter.3.cloned.1.call-done = bf16[128,1024]{1,0:T(8,128)(2,1)} async-done(((bf16[256,1024]{1,0:T(8,128)(2,1)}), bf16[128,1024]{1,0:T(8,128)(2,1)}) %reduce-scatter.3.cloned.1.call-update) | async-done | bytes 262160 | tf_op jit(solution)/shard_map/reduce_scatter | solution.py:98
  92.0 2.4 %scatter_custom_fusion = bf16[256,1024]{1,0:T(8,128)(2,1)} fusion(s32[128]{0:T(128)S(1)} %fusion.35, bf16[128,1024]{1,0:T(8,128)(2,1)} %reduce-scatter.3.cloned.1.call-done, bf16[]{:T(256)} %constant.42.clone.1), kind=kCustom, calls=%fused_computation.46 | custom fusion | bytes 524800 | tf_op jit(solution)/shard_map/scatter | solution.py:89
  94.3 5.6 %all-to-all-start.1 = ((bf16[16,16,1024]{2,1,0:T(8,128)(2,1)}), bf16[16,16,1024]{2,1,0:T(8,128)(2,1)S(1)}, u32[]{:S(2)}, u32[]{:S(2)}) async-start(bf16[16,16,1024]{2,1,0:T(8,128)(2,1)} %bitcast.12), calls=%async_computation.2 | async-start | bytes 1048576 | tf_op jit(solution)/shard_map/all_to_all | solution.py:101
  100.0 9.5 %reduce-scatter.5.cloned.1.call-done = bf16[128,1024]{1,0:T(8,128)(2,1)} async-done(((bf16[256,1024]{1,0:T(8,128)(2,1)}), bf16[128,1024]{1,0:T(8,128)(2,1)}) %reduce-scatter.5.cloned.1.call-update) | async-done | bytes 262160 | tf_op jit(solution)/shard_map/reduce_scatter | solution.py:107
  109.5 2.4 %scatter_custom_fusion.2 = bf16[256,1024]{1,0:T(8,128)(2,1)} fusion(s32[128]{0:T(128)S(1)} %fusion.35, bf16[128,1024]{1,0:T(8,128)(2,1)} %reduce-scatter.5.cloned.1.call-done, bf16[]{:T(256)} %constant.42.clone.1), kind=kCustom, calls=%fused_computation.44 | custom fusion | bytes 524800 | tf_op jit(solution)/shard_map/scatter | solution.py:89
  111.8 2.6 %all-to-all-done.1 = bf16[16,16,1024]{2,1,0:T(8,128)(2,1)S(1)} async-done(((bf16[16,16,1024]{2,1,0:T(8,128)(2,1)}), bf16[16,16,1024]{2,1,0:T(8,128)(2,1)S(1)}, u32[]{:S(2)}, u32[]{:S(2)}) %all-to-all-start.1) | async-done | bytes 524320 | tf_op jit(solution)/shard_map/all_to_all | solution.py:101
  114.4 4.1 %all-to-all-start.3 = ((bf16[16,16,1024]{2,1,0:T(8,128)(2,1)}), bf16[16,16,1024]{2,1,0:T(8,128)(2,1)S(1)}, u32[]{:S(2)}, u32[]{:S(2)}) async-start(bf16[16,16,1024]{2,1,0:T(8,128)(2,1)} %bitcast.16), calls=%async_computation.5 | async-start | bytes 1048576 | tf_op jit(solution)/shard_map/all_to_all | solution.py:110
  118.6 2.4 %fusion = bf16[1,512,1024]{2,1,0:T(8,128)(2,1)} fusion(bf16[256,512]{1,0:T(8,128)(2,1)} %get-tuple-element.14, bf16[256,1024]{1,0:T(8,128)(2,1)S(1)} %all_gather.6), kind=kOutput, calls=%fused_computation.11 | convolution fusion | flops 268959744 | bytes 1835008 | tf_op jit(solution)/shard_map/dot_general | solution.py:36
  121.1 1.4 fusion.1
  122.5 1.4 fusion.2
  123.9 3.0 %scatter_custom_fusion.1 = f32[128,1024]{1,0:T(8,128)S(1)} fusion(s32[256]{0:T(256)S(1)} %bitcast.86, bf16[256,1024]{1,0:T(8,128)(2,1)S(1)} %bitcast.83, f32[]{:T(128)} %constant.28.clone.1, f32[256]{0:T(256)S(1)} %mul.76, pred[256]{0:T(512)(128)(4,1)S(1)} %gt.25), kind=kCustom, calls=%fused_computation.21 | custom fusion | flops 1048576 | bytes 1051136 | tf_op jit(solution)/shard_map/scatter-add | solution.py:122
  127.6 5.4 %all-to-all-done.3 = bf16[16,16,1024]{2,1,0:T(8,128)(2,1)S(1)} async-done(((bf16[16,16,1024]{2,1,0:T(8,128)(2,1)}), bf16[16,16,1024]{2,1,0:T(8,128)(2,1)S(1)}, u32[]{:S(2)}, u32[]{:S(2)}) %all-to-all-start.3) | async-done | bytes 524320 | tf_op jit(solution)/shard_map/all_to_all | solution.py:110
  133.0 2.9 %scatter_custom_fusion.3 = f32[128,1024]{1,0:T(8,128)S(1)} fusion(s32[256]{0:T(256)S(1)} %bitcast.87, bf16[256,1024]{1,0:T(8,128)(2,1)S(1)} %bitcast.84, f32[]{:T(128)} %constant.28.clone.1, pred[256]{0:T(512)(128)(4,1)S(1)} %gt.25), kind=kCustom, calls=%fused_computation.18 | custom fusion | flops 786432 | bytes 1050112 | tf_op jit(solution)/shard_map/scatter-add | solution.py:131
  (47 shorter events, 12.1 us)
Async XLA Ops:
  7.2 67.4 %copy-start = (bf16[1,512,1024]{2,1,0:T(8,128)(2,1)S(1)}, bf16[1,512,1024]{2,1,0:T(8,128)(2,1)}, u32[]{:S(2)}) copy-start(bf16[1,512,1024]{2,1,0:T(8,128)(2,1)} %param.17) | copy-start | bytes 3145732
  13.3 8.5 %copy-start.1 = (bf16[128,1024]{1,0:T(8,128)(2,1)S(1)}, bf16[128,1024]{1,0:T(8,128)(2,1)}, u32[]{:S(2)}) copy-start(bf16[128,1024]{1,0:T(8,128)(2,1)} %param.11) | copy-start | bytes 786436
  14.3 21.9 %all-to-all-start.2 = ((bf16[16,16,1024]{2,1,0:T(8,128)(2,1)}), bf16[16,16,1024]{2,1,0:T(8,128)(2,1)S(1)}, u32[]{:S(2)}, u32[]{:S(2)}) async-start(bf16[16,16,1024]{2,1,0:T(8,128)(2,1)} %bitcast.14), calls=%async_computation.3 | async-start | bytes 1048576 | tf_op jit(solution)/shard_map/all_to_all | solution.py:102
  36.2 18.6 %all-to-all-start = ((bf16[16,16,1024]{2,1,0:T(8,128)(2,1)}), bf16[16,16,1024]{2,1,0:T(8,128)(2,1)S(1)}, u32[]{:S(2)}, u32[]{:S(2)}) async-start(bf16[16,16,1024]{2,1,0:T(8,128)(2,1)} %bitcast.7), calls=%async_computation | async-start | bytes 1048576 | tf_op jit(solution)/shard_map/all_to_all | solution.py:94
  40.3 51.7 %reduce-scatter.3.cloned.1.call-start = ((), (), s32[]{:S(2)}) async-start(), calls=%async_computation.6 | async-start | bytes 786432 | tf_op jit(solution)/shard_map/reduce_scatter | solution.py:98
  55.6 9.2 %copy-start.2 = (bf16[1,512,1024]{2,1,0:T(8,128)(2,1)S(1)}, bf16[1,512,1024]{2,1,0:T(8,128)(2,1)}, u32[]{:S(2)}) copy-start(bf16[1,512,1024]{2,1,0:T(8,128)(2,1)} %param.15) | copy-start | bytes 3145732
  64.8 1.2 copy-start.3
  77.3 32.2 %reduce-scatter.5.cloned.1.call-start = ((), (), s32[]{:S(2)}) async-start(), calls=%async_computation.7 | async-start | bytes 786432 | tf_op jit(solution)/shard_map/reduce_scatter | solution.py:107
  77.3 1.5 %copy-start.4 = (bf16[1,512,1024]{2,1,0:T(8,128)(2,1)S(1)}, bf16[1,512,1024]{2,1,0:T(8,128)(2,1)}, u32[]{:S(2)}) copy-start(bf16[1,512,1024]{2,1,0:T(8,128)(2,1)} %param.16) | copy-start | bytes 3145732
  77.3 1.5 %copy-start.5 = (bf16[256,512]{1,0:T(8,128)(2,1)S(1)}, bf16[256,512]{1,0:T(8,128)(2,1)}, u32[]{:S(2)}) copy-start(bf16[256,512]{1,0:T(8,128)(2,1)} %get-tuple-element.13) | copy-start | bytes 786436
  94.3 20.1 %all-to-all-start.1 = ((bf16[16,16,1024]{2,1,0:T(8,128)(2,1)}), bf16[16,16,1024]{2,1,0:T(8,128)(2,1)S(1)}, u32[]{:S(2)}, u32[]{:S(2)}) async-start(bf16[16,16,1024]{2,1,0:T(8,128)(2,1)} %bitcast.12), calls=%async_computation.2 | async-start | bytes 1048576 | tf_op jit(solution)/shard_map/all_to_all | solution.py:101
  114.4 18.6 %all-to-all-start.3 = ((bf16[16,16,1024]{2,1,0:T(8,128)(2,1)}), bf16[16,16,1024]{2,1,0:T(8,128)(2,1)S(1)}, u32[]{:S(2)}, u32[]{:S(2)}) async-start(bf16[16,16,1024]{2,1,0:T(8,128)(2,1)} %bitcast.16), calls=%async_computation.5 | async-start | bytes 1048576 | tf_op jit(solution)/shard_map/all_to_all | solution.py:110
  118.6 2.4 %copy-start.6 = (bf16[256,512]{1,0:T(8,128)(2,1)S(1)}, bf16[256,512]{1,0:T(8,128)(2,1)}, u32[]{:S(2)}) copy-start(bf16[256,512]{1,0:T(8,128)(2,1)} %get-tuple-element.13) | copy-start | bytes 786436
Sparse Core Ops, SparseCore 0:
  77.4 14.5 reduce-scatter.2
  94.9 14.5 reduce-scatter.4
where the time goes:
time: 144 us; the launch traced here: 143 us
  waiting for transfers between devices  55 us (38%)
  starting transfers between devices  21.3 us (15%)
  blocking collectives  17.1 us (12%)
  between operations  14.3 us (10%)
  other arithmetic  12.9 us (9%)
  matrix products  11.6 us (8%)
  local copies, waits for them, and re-layouts  11.3 us (8%)
    all_to_all x1, waiting for transfers between devices, per_device(): lax.all_to_all(row_send, 'expert', split_axis=0, concat_axis=0, tiled=True)  13.3 us
    all_to_all x1, waiting for transfers between devices, per_device(): lax.all_to_all(grad_send, 'expert', split_axis=0, concat_axis=0, tiled=True)  12.4 us
    reduce_scatter x1, waiting for transfers between devices, per_device(): lax.psum_scatter(out_part.astype(jnp.bfloat16), 'dp', scatter_dimension=0...  11.8 us
    reduce_scatter x1, waiting for transfers between devices, per_device(): lax.psum_scatter(back_part.astype(jnp.bfloat16), 'dp', scatter_dimension=...  9.49 us
    all_gather x1, blocking collectives, per_device(): row_block = lax.all_gather(compact(recv_rows), 'dp', axis=0, tiled=True)  9.04 us
    all_gather x1, blocking collectives, per_device(): grad_block = lax.all_gather(compact(recv_grads), 'dp', axis=0, tiled=True)  8.06 us
    all_to_all x1, starting transfers between devices, per_device(): lax.all_to_all(grad_send, 'expert', split_axis=0, concat_axis=0, tiled=True)  7.39 us
    all_to_all x1, starting transfers between devices, per_device(): lax.all_to_all(expand(out_rows), 'expert', split_axis=0, concat_axis=0, t...  5.62 us
  transfers between devices with their start and end apart: 6, of which 6 were waited for; matrix products, arithmetic and copies ran while one was open for 14% of the time, Pallas kernels for 0%

commit v1 on v0

v1 whole, which is shorter than its diff:
```python
import functools

import jax
import jax.numpy as jnp
from jax import lax
from jax.experimental import pallas as pl
from jax.experimental.pallas import tpu as pltpu
from jax.sharding import PartitionSpec as P

MESH = pl.DeviceIdType.MESH
BF16 = jnp.bfloat16
F32 = jnp.float32
NN = (((1,), (0,)), ((), ()))
NT = (((1,), (1,)), ((), ()))
TN = (((0,), (0,)), ((), ()))


def dot(a, b, dims=NN):
    return lax.dot_general(a, b, dims, preferred_element_type=F32)


def layer_kernel(
    n_dp, n_e, n_c, slot_rows,
    tok_ref, cot_ref, list_ref, comb_ref, wg_hbm, wu_hbm, wd_hbm,
    out_ref, back_ref, gg_hbm, gu_hbm, gd_hbm,
    list_two, comb_two, wg, wu, wd, gg, gu, gd,
    send, recv, rows, part_send, part_own, part_recv, ret_send, ret_recv,
    gate_acc, up_acc, hid, dgate, dup,
    w_sem, g_sem, a2a_ss, a2a_rs, x_ss, x_rs, red_ss, red_rs, ret_ss, ret_rs,
):
    my_dp = lax.axis_index("dp")
    me = lax.axis_index("expert")
    tok_rows, feat = tok_ref.shape
    capacity = list_ref.shape[1]
    ff = wg.shape[0]
    width = feat // n_c
    peers = n_e - 1
    others = n_dp - 1
    padded = n_e * slot_rows
    sent = peers * slot_rows

    barrier = pltpu.get_barrier_semaphore()

    def greet_expert(k, carry):
        pl.semaphore_signal(
            barrier, inc=1, device_id=(my_dp, lax.rem(me + 1 + k, n_e)), device_id_type=MESH
        )
        return carry

    lax.fori_loop(0, peers, greet_expert, 0)
    for q in range(others):
        pl.semaphore_signal(
            barrier, inc=1, device_id=(lax.rem(my_dp + 1 + q, n_dp), me), device_id_type=MESH
        )

    loads = [
        pltpu.make_async_copy(hbm, vmem, w_sem.at[i])
        for i, (hbm, vmem) in enumerate(((wg_hbm, wg), (wu_hbm, wu), (wd_hbm, wd)))
    ]
    for load in loads:
        load.start()

    list_two[0:n_e, :] = list_ref[...]
    list_two[n_e : 2 * n_e, :] = list_ref[...]
    comb_two[0:n_e, :] = comb_ref[...]
    comb_two[n_e : 2 * n_e, :] = comb_ref[...]
    copies = max(1, 128 // n_e)
    list_rel = list_two[pl.ds(me + 1, n_e), :].astype(F32)
    comb_rel = comb_two[pl.ds(me + 1, n_e), :]
    list_t = jnp.concatenate([list_rel] * copies, axis=0).T
    comb_t = jnp.concatenate([comb_rel] * copies, axis=0).T
    base = (me * tok_rows).astype(F32)
    token_id = lax.broadcasted_iota(jnp.int32, (1, tok_rows), 1).astype(F32) + base
    member_rows, weight_rows = [], []
    for k in range(n_e):
        same = list_t[:, k : k + 1] == token_id
        member_rows.append(jnp.sum(jnp.where(same, 1.0, 0.0), axis=0, keepdims=True))
        weight_rows.append(
            jnp.sum(jnp.where(same, comb_t[:, k : k + 1], 0.0), axis=0, keepdims=True)
        )
    member = jnp.concatenate(member_rows, axis=0)
    t_from = lax.broadcasted_iota(jnp.int32, (tok_rows, tok_rows), 0)
    t_to = lax.broadcasted_iota(jnp.int32, (tok_rows, tok_rows), 1)
    before = jnp.where(t_from < t_to, 1.0, 0.0).astype(BF16)
    rank = dot(member.astype(BF16), before)
    rank = jnp.where(member > 0.0, rank, -1.0)
    slot_id = lax.broadcasted_iota(jnp.int32, (slot_rows, tok_rows), 0).astype(F32)
    hits = [slot_id == rank[k : k + 1, :] for k in range(n_e)]
    pick = jnp.concatenate([jnp.where(h, 1.0, 0.0) for h in hits], axis=0)
    pick_w = jnp.concatenate(
        [jnp.where(h, weight_rows[k], 0.0) for k, h in enumerate(hits)], axis=0
    )
    pick_b = pick.astype(BF16)
    row_weight = jnp.sum(pick_w, axis=1, keepdims=True)

    def to_experts(a, c):
        def step(k, carry):
            span = pl.ds(pl.multiple_of(k * slot_rows, 16), slot_rows)
            pltpu.make_async_remote_copy(
                src_ref=send.at[a, c, span],
                dst_ref=recv.at[a, c, span],
                send_sem=a2a_ss.at[a, c],
                recv_sem=a2a_rs.at[a, c],
                device_id=(my_dp, lax.rem(me + 1 + k, n_e)),
                device_id_type=MESH,
            ).start()
            return carry

        lax.fori_loop(0, peers, step, 0)

    def to_sources(a, c):
        def step(k, carry):
            span = pl.ds(pl.multiple_of(k * slot_rows, 16), slot_rows)
            pltpu.make_async_remote_copy(
                src_ref=ret_send.at[a, c, span],
                dst_ref=ret_recv.at[a, c, span],
                send_sem=ret_ss.at[a, c],
                recv_sem=ret_rs.at[a, c],
                device_id=(my_dp, lax.rem(me + (n_e - 1) - k, n_e)),
                device_id_type=MESH,
            ).start()
            return carry

        lax.fori_loop(0, peers, step, 0)

    def whole(src, dst, ss, rs, a, c, count):
        return pltpu.make_async_remote_copy(
            src_ref=src.at[a, c, 0:count],
            dst_ref=dst.at[a, c, 0:count],
            send_sem=ss.at[a, c],
            recv_sem=rs.at[a, c],
            device_id=(my_dp, lax.rem(me + 1, n_e)),
            device_id_type=MESH,
        )

    def a2a_all(a, c):
        return whole(send, recv, a2a_ss, a2a_rs, a, c, sent)

    def ret_all(a, c):
        return whole(ret_send, ret_recv, ret_ss, ret_rs, a, c, sent)

    def x_all(a, c):
        return whole(rows, rows, x_ss, x_rs, a, c, others * capacity)

    def red_all(a, c):
        return whole(part_send, part_recv, red_ss, red_rs, a, c, others * capacity)

    for a in range(2):
        for c in range(n_c):
            cols = slice(c * width, (c + 1) * width)
            if a == 0:
                block = dot(pick_b, tok_ref[:, cols]).astype(BF16)
            else:
                block = (row_weight * dot(pick_b, cot_ref[:, cols])).astype(BF16)
            send[a, c] = block[0:sent]
            recv[a, c, sent:padded] = block[sent:padded]
            if a == 0 and c == 0:
                pl.semaphore_wait(barrier, peers + others)
            to_experts(a, c)

    lane = lax.broadcasted_iota(jnp.int32, (1, padded), 1).astype(F32)
    lane_k = jnp.floor((lane + 0.5) * (1.0 / slot_rows))
    lane_s = lane - lane_k * slot_rows
    source = me.astype(F32) - 1.0 - lane_k
    source = jnp.where(source < 0.0, source + n_e, source)
    own_list = list_t[:, n_e - 1 : n_e]
    low = source * tok_rows
    first = jnp.sum(jnp.where(own_list < low, 1.0, 0.0), axis=0, keepdims=True)
    last = jnp.sum(jnp.where(own_list < low + tok_rows, 1.0, 0.0), axis=0, keepdims=True)
    place = jnp.where(lane_s < last - first, first + lane_s, -1.0)
    row_id = lax.broadcasted_iota(jnp.int32, (capacity, padded), 0).astype(F32)
    pack = jnp.where(row_id == place, 1.0, 0.0)
    pack_b = pack.astype(BF16)
    unpack_b = pack.T.astype(BF16)
    pick_t = pick.T.astype(BF16)
    pick_wt = pick_w.T
    wt_high = pick_wt.astype(BF16)
    wt_low = (pick_wt - wt_high.astype(F32)).astype(BF16)

    def share(a, c):
        a2a_all(a, c).wait_recv()
        rows[a, c, others * capacity :] = dot(pack_b, recv[a, c]).astype(BF16)
        for q in range(others):
            pltpu.make_async_remote_copy(
                src_ref=rows.at[a, c, pl.ds(others * capacity, capacity)],
                dst_ref=rows.at[a, c, pl.ds(q * capacity, capacity)],
                send_sem=x_ss.at[a, c],
                recv_sem=x_rs.at[a, c],
                device_id=(lax.rem(my_dp + 1 + q, n_dp), me),
                device_id_type=MESH,
            ).start()

    def reduce_start(a, c, part):
        part = part.astype(BF16)
        part_send[a, c] = part[0 : others * capacity]
        part_own[a, c] = part[others * capacity :]
        for q in range(others):
            pltpu.make_async_remote_copy(
                src_ref=part_send.at[a, c, pl.ds(q * capacity, capacity)],
                dst_ref=part_recv.at[a, c, pl.ds(q * capacity, capacity)],
                send_sem=red_ss.at[a, c],
                recv_sem=red_rs.at[a, c],
                device_id=(lax.rem(my_dp + (n_dp - 1) - q, n_dp), me),
                device_id_type=MESH,
            ).start()

    def give_back(a, c):
        red_all(a, c).wait_recv()
        total = part_own[a, c].astype(F32)
        for q in range(others):
            total = total + part_recv[a, c, q * capacity : (q + 1) * capacity].astype(F32)
        slots = dot(unpack_b, total.astype(BF16)).astype(BF16)
        ret_send[a, c] = slots[0:sent]
        ret_recv[a, c, sent:padded] = slots[sent:padded]
        to_sources(a, c)

    h_step = min(256, ff)
    h_cuts = [slice(h, h + h_step) for h in range(0, ff, h_step)]

    for c in range(n_c):
        share(0, c)
    for load in loads:
        load.wait()
    for c in range(n_c):
        x_all(0, c).wait_recv()
        cols = slice(c * width, (c + 1) * width)
        for h in h_cuts:
            gate = dot(rows[0, c], wg[h, cols], NT)
            up = dot(rows[0, c], wu[h, cols], NT)
            if c > 0:
                gate = gate + gate_acc[:, h]
                up = up + up_acc[:, h]
            if c < n_c - 1:
                gate_acc[:, h] = gate
                up_acc[:, h] = up
            else:
                sigma = jax.nn.sigmoid(gate)
                silu = gate * sigma
                hid[:, h] = (silu * up).astype(BF16)
                gate_acc[:, h] = up * sigma * (1.0 + gate * (1.0 - sigma))
                up_acc[:, h] = silu
    for c in range(n_c):
        reduce_start(0, c, dot(hid[...], wd[:, c * width : (c + 1) * width]))
    share(1, 0)
    give_back(0, 0)
    for c in range(1, n_c):
        share(1, c)
        give_back(0, c)

    for h in h_cuts:
        d_hidden = None
        for c in range(n_c):
            if h.start == 0:
                x_all(1, c).wait_recv()
            term = dot(rows[1, c], wd[h, c * width : (c + 1) * width], NT)
            d_hidden = term if d_hidden is None else d_hidden + term
        dgate[:, h] = (d_hidden * gate_acc[:, h]).astype(BF16)
        dup[:, h] = (d_hidden * up_acc[:, h]).astype(BF16)
    for c in range(n_c):
        cols = slice(c * width, (c + 1) * width)
        reduce_start(1, c, dot(dgate[...], wg[:, cols]) + dot(dup[...], wu[:, cols]))

    def weight_grad(c, left, a, grad):
        cols = slice(c * width, (c + 1) * width)
        for h in h_cuts:
            grad[h, cols] = dot(left[:, h], rows[a, c], TN).astype(BF16)

    stores = [
        pltpu.make_async_copy(vmem, hbm, g_sem.at[i])
        for i, (vmem, hbm) in enumerate(((gg, gg_hbm), (gu, gu_hbm), (gd, gd_hbm)))
    ]
    for c in range(n_c):
        weight_grad(c, hid, 1, gd)
    stores[2].start()
    for c in range(n_c):
        give_back(1, c)
    for c in range(n_c):
        weight_grad(c, dgate, 0, gg)
    stores[0].start()
    for c in range(n_c):
        weight_grad(c, dup, 0, gu)
    stores[1].start()

    for c in range(n_c):
        cols = slice(c * width, (c + 1) * width)
        ret_all(0, c).wait_recv()
        got = ret_recv[0, c]
        out_ref[:, cols] = (dot(wt_high, got) + dot(wt_low, got)).astype(BF16)
    for c in range(n_c):
        cols = slice(c * width, (c + 1) * width)
        ret_all(1, c).wait_recv()
        back_ref[:, cols] = dot(pick_t, ret_recv[1, c]).astype(BF16)
    for store in stores:
        store.wait()
    for a in range(2):
        for c in range(n_c):
            a2a_all(a, c).wait_send()
            x_all(a, c).wait_send()
            red_all(a, c).wait_send()
            ret_all(a, c).wait_send()


def per_device(n_dp, n_e, tokens, cotangent, pick_lists, combine, w_gate, w_up, w_down):
    tok_rows, feat = tokens.shape
    capacity = pick_lists.shape[2]
    ff = w_gate.shape[1]
    slot_count = max(2, (2 * capacity + n_e - 1) // n_e)
    slot_rows = (slot_count + 15) // 16 * 16
    n_c = 2
    width = feat // n_c
    padded = n_e * slot_rows
    sent = padded - slot_rows
    total_rows = n_dp * capacity
    other_rows = total_rows - capacity
    vmem = pl.BlockSpec(memory_space=pltpu.VMEM)
    hbm = pl.BlockSpec(memory_space=pl.ANY)
    grad = jax.ShapeDtypeStruct((ff, feat), BF16)
    sems = pltpu.SemaphoreType.DMA((2, n_c))
    outs = pl.pallas_call(
        functools.partial(layer_kernel, n_dp, n_e, n_c, slot_rows),
        out_shape=(
            jax.ShapeDtypeStruct((tok_rows, feat), BF16),
            jax.ShapeDtypeStruct((tok_rows, feat), BF16),
            grad,
            grad,
            grad,
        ),
        in_specs=[vmem] * 4 + [hbm] * 3,
        out_specs=(vmem, vmem, hbm, hbm, hbm),
        scratch_shapes=[
            pltpu.VMEM((2 * n_e, capacity), jnp.int32),
            pltpu.VMEM((2 * n_e, capacity), F32),
        ]
        + [pltpu.VMEM((ff, feat), BF16)] * 6
        + [
            pltpu.VMEM((2, n_c, sent, width), BF16),
            pltpu.VMEM((2, n_c, padded, width), BF16),
            pltpu.VMEM((2, n_c, total_rows, width), BF16),
            pltpu.VMEM((2, n_c, other_rows, width), BF16),
            pltpu.VMEM((2, n_c, capacity, width), BF16),
            pltpu.VMEM((2, n_c, other_rows, width), BF16),
            pltpu.VMEM((2, n_c, sent, width), BF16),
            pltpu.VMEM((2, n_c, padded, width), BF16),
            pltpu.VMEM((total_rows, ff), F32),
            pltpu.VMEM((total_rows, ff), F32),
        ]
        + [pltpu.VMEM((total_rows, ff), BF16)] * 3
        + [pltpu.SemaphoreType.DMA((3,))] * 2
        + [sems] * 8,
        compiler_params=pltpu.CompilerParams(
            collective_id=0, has_side_effects=True, vmem_limit_bytes=56 * 2**20
        ),
        cost_estimate=pl.CostEstimate(
            flops=18 * total_rows * ff * feat,
            bytes_accessed=12 * ff * feat + 8 * tok_rows * feat,
            transcendentals=total_rows * ff,
        ),
        name="expert_layer",
    )(tokens, cotangent, pick_lists[0], combine[0], w_gate[0], w_up[0], w_down[0])
    layer_out, tokens_grad, grad_gate, grad_up, grad_down = outs
    return (layer_out, tokens_grad, grad_gate[None], grad_up[None], grad_down[None])


def solution(mesh):
    placed = (
        P(("dp", "expert"), None),
        P(("dp", "expert"), None),
        P("dp", None, None),
        P("dp", None, None),
        P("expert", "dp", None),
        P("expert", "dp", None),
        P("expert", "dp", None),
    )
    return jax.shard_map(
        functools.partial(per_device, mesh.shape["dp"], mesh.shape["expert"]),
        mesh=mesh,
        in_specs=placed,
        out_specs=(
            P(("dp", "expert"), None),
            P(("dp", "expert"), None),
            P("expert", "dp", None),
            P("expert", "dp", None),
            P("expert", "dp", None),
        ),
        check_vma=False,
    )
```

time: 144 us -> 68.1 us (0.47)
  Pallas kernels: 0 us -> 59.6 us
  waiting for transfers between devices: 55 us -> 0 us
  starting transfers between devices: 21.3 us -> 0 us
  blocking collectives: 17.1 us -> 0 us
  between operations: 14.3 us -> 0.65 us
  other arithmetic: 12.9 us -> 0 us
  matrix products: 11.6 us -> 0 us
  local copies, waits for them, and re-layouts: 11.3 us -> 7.6 us
    pallas_call x0 -> x1, Pallas kernels: none -> 59.6 us  [per_device(): pl.pallas_call(functools.partial(layer_kernel, n_dp, n_e, n_c, slot_rows)...]
    all_to_all x4 -> x0, waiting for transfers between devices: 33.7 us -> none  [the longest x1 13.3 us: per_device(): lax.all_to_all(row_send, 'expert', split_axis=0, concat_axis=0, tiled=True)]
    reduce_scatter x2 -> x0, waiting for transfers between devices: 21.3 us -> none  [the longest x1 11.8 us: per_device(): lax.psum_scatter(out_part.astype(jnp.bfloat16), 'dp', scatter_dimension=0...]
    all_to_all x4 -> x0, starting transfers between devices: 21.2 us -> none  [the longest x1 7.39 us: per_device(): lax.all_to_all(grad_send, 'expert', split_axis=0, concat_axis=0, tiled=True)]
    all_gather x2 -> x0, blocking collectives: 17.1 us -> none  [the longest x1 9.04 us: per_device(): row_block = lax.all_gather(compact(recv_rows), 'dp', axis=0, tiled=True)]
    dot_general x9 -> x0, matrix products: 11.6 us -> none  [the longest x1 2.42 us: weight_grads(): lax.dot_general(d_gate, row_block, dims, preferred_element_type=jnp.float32)]
    unnamed x14 -> x11, local copies, waits for them, and re-layouts: 0.79 us -> 7.6 us
    scatter-add x2 -> x0, other arithmetic: 5.86 us -> none  [the longest x1 2.97 us: per_device(): layer_out = jnp.zeros((tok_rows, feat_width), jnp.float32).at[flat_row].a...]
  transfers between devices with their start and end apart: 6 -> 0, of which waited for: 6 -> 0; matrix products, arithmetic and copies ran while one was open for 14% -> 0% of each run, Pallas kernels for 0% -> 0%
where the time goes in v1:
time: 68.1 us; the launch traced here: 67.8 us
  Pallas kernels  59.6 us (88%)
  local copies, waits for them, and re-layouts  7.6 us (11%)
    pallas_call x1, Pallas kernels, per_device(): pl.pallas_call(functools.partial(layer_kernel, n_dp, n_e, n_c, slot_rows)...  59.6 us
    unnamed x11, local copies, waits for them, and re-layouts  7.6 us

profile of v1, /device:TPU:0, one launch (start us, length us, event | category | flops | bytes accessed | tf_op | source)
XLA Modules:
  0.0 67.8 jit_solution(3813964027574873246)
XLA Ops:
  0.6 59.6 %expert_layer.1 = (bf16[128,1024]{1,0:T(8,128)(2,1)}, bf16[128,1024]{1,0:T(8,128)(2,1)}, bf16[512,1024]{1,0:T(8,128)(2,1)}, bf16[512,1024]{1,0:T(8,128)(2,1)}, bf16[512,1024]{1,0:T(8,128)(2,1)}) custom-call(bf16[128,1024]{1,0:T(8,128)(2,1)} %tok_ref.1, bf16[128,1024]{1,0:T(8,128)(2,1)} %cot_ref.1, s32[16,128]{1,0:T(8,128)} %bitcast.14, f32[16,128]{1,0:T(8,128)} %bitcast.15, ...), custom_call_target="tpu_custom_call" | custom-call | flops 2415919104 | bytes 7340032 | tf_op jit(solution)/shard_map/expert_layer/pallas_call | solution.py:319
  60.2 0.0 copy-start.2
  60.2 1.8 %copy.17 = bf16[128,1024]{1,0:T(8,128)(2,1)} copy(bf16[128,1024]{1,0:T(8,128)(2,1)} %get-tuple-element.20) | data formatting | bytes 524288
  62.0 1.7 %copy.18 = bf16[128,1024]{1,0:T(8,128)(2,1)} copy(bf16[128,1024]{1,0:T(8,128)(2,1)} %get-tuple-element.21) | data formatting | bytes 524288
  63.7 0.0 copy-done.2
  63.7 0.0 copy-start.1
  63.7 1.0 %copy.19 = bf16[1,512,1024]{2,1,0:T(8,128)(2,1)} copy(bf16[1,512,1024]{2,1,0:T(8,128)(2,1)S(1)} %bitcast.10) | data formatting | bytes 2097152
  64.6 0.6 copy-done.1
  65.3 0.0 copy-start
  65.3 1.0 %copy.20 = bf16[1,512,1024]{2,1,0:T(8,128)(2,1)} copy(bf16[1,512,1024]{2,1,0:T(8,128)(2,1)S(1)} %bitcast.9) | data formatting | bytes 2097152
  66.2 0.6 copy-done
  66.9 1.0 %copy.21 = bf16[1,512,1024]{2,1,0:T(8,128)(2,1)} copy(bf16[1,512,1024]{2,1,0:T(8,128)(2,1)S(1)} %bitcast.8) | data formatting | bytes 2097152
Async XLA Ops:
  60.2 3.4 %copy-start.2 = (bf16[512,1024]{1,0:T(8,128)(2,1)S(1)}, bf16[512,1024]{1,0:T(8,128)(2,1)}, u32[]{:S(2)}) copy-start(bf16[512,1024]{1,0:T(8,128)(2,1)} %get-tuple-element.12) | copy-start | bytes 3145732
  63.7 1.6 %copy-start.1 = (bf16[512,1024]{1,0:T(8,128)(2,1)S(1)}, bf16[512,1024]{1,0:T(8,128)(2,1)}, u32[]{:S(2)}) copy-start(bf16[512,1024]{1,0:T(8,128)(2,1)} %get-tuple-element.13) | copy-start | bytes 3145732
  65.3 1.6 %copy-start = (bf16[512,1024]{1,0:T(8,128)(2,1)S(1)}, bf16[512,1024]{1,0:T(8,128)(2,1)}, u32[]{:S(2)}) copy-start(bf16[512,1024]{1,0:T(8,128)(2,1)} %get-tuple-element.14) | copy-start | bytes 3145732

commit v2 on v1

--- a/solution.py
+++ b/solution.py
@@ -21,17 +21,17 @@
 
 def layer_kernel(
     n_dp, n_e, n_c, slot_rows,
-    tok_ref, cot_ref, list_ref, comb_ref, wg_hbm, wu_hbm, wd_hbm,
-    out_ref, back_ref, gg_hbm, gu_hbm, gd_hbm,
-    list_two, comb_two, wg, wu, wd, gg, gu, gd,
+    tok_hbm, cot_hbm, list_hbm, comb_hbm, wg_hbm, wu_hbm, wd_hbm,
+    out_ref, back_ref, gg, gu, gd,
+    list_two, comb_two, tok_ref, cot_ref, wg, wu, wd,
     send, recv, rows, part_send, part_own, part_recv, ret_send, ret_recv,
     gate_acc, up_acc, hid, dgate, dup,
-    w_sem, g_sem, a2a_ss, a2a_rs, x_ss, x_rs, red_ss, red_rs, ret_ss, ret_rs,
+    w_sem, a2a_ss, a2a_rs, x_ss, x_rs, red_ss, red_rs, ret_ss, ret_rs,
 ):
     my_dp = lax.axis_index("dp")
     me = lax.axis_index("expert")
     tok_rows, feat = tok_ref.shape
-    capacity = list_ref.shape[1]
+    capacity = list_two.shape[1]
     ff = wg.shape[0]
     width = feat // n_c
     peers = n_e - 1
@@ -53,17 +53,28 @@
             barrier, inc=1, device_id=(lax.rem(my_dp + 1 + q, n_dp), me), device_id_type=MESH
         )
 
+    early = [
+        pltpu.make_async_copy(hbm, vmem, w_sem.at[i])
+        for i, (hbm, vmem) in enumerate(
+            (
+                (list_hbm, list_two.at[pl.ds(0, n_e)]),
+                (list_hbm, list_two.at[pl.ds(n_e, n_e)]),
+                (comb_hbm, comb_two.at[pl.ds(0, n_e)]),
+                (comb_hbm, comb_two.at[pl.ds(n_e, n_e)]),
+                (tok_hbm, tok_ref),
+                (cot_hbm, cot_ref),
+            )
+        )
+    ]
     loads = [
-        pltpu.make_async_copy(hbm, vmem, w_sem.at[i])
+        pltpu.make_async_copy(hbm, vmem, w_sem.at[6 + i])
         for i, (hbm, vmem) in enumerate(((wg_hbm, wg), (wu_hbm, wu), (wd_hbm, wd)))
     ]
-    for load in loads:
+    for load in early + loads:
         load.start()
-
-    list_two[0:n_e, :] = list_ref[...]
-    list_two[n_e : 2 * n_e, :] = list_ref[...]
-    comb_two[0:n_e, :] = comb_ref[...]
-    comb_two[n_e : 2 * n_e, :] = comb_ref[...]
+    for load in early[:4]:
+        load.wait()
+
     copies = max(1, 128 // n_e)
     list_rel = list_two[pl.ds(me + 1, n_e), :].astype(F32)
     comb_rel = comb_two[pl.ds(me + 1, n_e), :]
@@ -94,7 +105,8 @@
     row_weight = jnp.sum(pick_w, axis=1, keepdims=True)
 
     def to_experts(a, c):
-        def step(k, carry):
+        def step(i, carry):
+            k = lax.rem(i * (peers // 2), peers)
             span = pl.ds(pl.multiple_of(k * slot_rows, 16), slot_rows)
             pltpu.make_async_remote_copy(
                 src_ref=send.at[a, c, span],
@@ -109,7 +121,8 @@
         lax.fori_loop(0, peers, step, 0)
 
     def to_sources(a, c):
-        def step(k, carry):
+        def step(i, carry):
+            k = lax.rem(i * (peers // 2), peers)
             span = pl.ds(pl.multiple_of(k * slot_rows, 16), slot_rows)
             pltpu.make_async_remote_copy(
                 src_ref=ret_send.at[a, c, span],
@@ -145,18 +158,24 @@
     def red_all(a, c):
         return whole(part_send, part_recv, red_ss, red_rs, a, c, others * capacity)
 
-    for a in range(2):
-        for c in range(n_c):
-            cols = slice(c * width, (c + 1) * width)
-            if a == 0:
-                block = dot(pick_b, tok_ref[:, cols]).astype(BF16)
-            else:
-                block = (row_weight * dot(pick_b, cot_ref[:, cols])).astype(BF16)
-            send[a, c] = block[0:sent]
-            recv[a, c, sent:padded] = block[sent:padded]
-            if a == 0 and c == 0:
-                pl.semaphore_wait(barrier, peers + others)
-            to_experts(a, c)
+    def dispatch(a, c):
+        cols = slice(c * width, (c + 1) * width)
+        if a == 0:
+            block = dot(pick_b, tok_ref[:, cols]).astype(BF16)
+        else:
+            block = (row_weight * dot(pick_b, cot_ref[:, cols])).astype(BF16)
+        send[a, c] = block[0:sent]
+        recv[a, c, sent:padded] = block[sent:padded]
+        if a == 0 and c == 0:
+            pl.semaphore_wait(barrier, peers + others)
+        to_experts(a, c)
+
+    early[4].wait()
+    for c in range(n_c):
+        dispatch(0, c)
+    early[5].wait()
+    for c in range(2):
+        dispatch(1, c)
 
     lane = lax.broadcasted_iota(jnp.int32, (1, padded), 1).astype(F32)
     lane_k = jnp.floor((lane + 0.5) * (1.0 / slot_rows))
@@ -219,6 +238,8 @@
 
     for c in range(n_c):
         share(0, c)
+        if c + 2 < n_c:
+            dispatch(1, c + 2)
     for load in loads:
         load.wait()
     for c in range(n_c):
@@ -265,21 +286,14 @@
         for h in h_cuts:
             grad[h, cols] = dot(left[:, h], rows[a, c], TN).astype(BF16)
 
-    stores = [
-        pltpu.make_async_copy(vmem, hbm, g_sem.at[i])
-        for i, (vmem, hbm) in enumerate(((gg, gg_hbm), (gu, gu_hbm), (gd, gd_hbm)))
-    ]
     for c in range(n_c):
         weight_grad(c, hid, 1, gd)
-    stores[2].start()
     for c in range(n_c):
         give_back(1, c)
     for c in range(n_c):
         weight_grad(c, dgate, 0, gg)
-    stores[0].start()
     for c in range(n_c):
         weight_grad(c, dup, 0, gu)
-    stores[1].start()
 
     for c in range(n_c):
         cols = slice(c * width, (c + 1) * width)
@@ -290,8 +304,6 @@
         cols = slice(c * width, (c + 1) * width)
         ret_all(1, c).wait_recv()
         back_ref[:, cols] = dot(pick_t, ret_recv[1, c]).astype(BF16)
-    for store in stores:
-        store.wait()
     for a in range(2):
         for c in range(n_c):
             a2a_all(a, c).wait_send()
@@ -300,13 +312,22 @@
             ret_all(a, c).wait_send()
 
 
+def store_kernel(*refs):
+    sem = refs[10]
+    copies = [pltpu.make_async_copy(refs[i], refs[5 + i], sem.at[i]) for i in range(5)]
+    for copy in copies:
+        copy.start()
+    for copy in copies:
+        copy.wait()
+
+
 def per_device(n_dp, n_e, tokens, cotangent, pick_lists, combine, w_gate, w_up, w_down):
     tok_rows, feat = tokens.shape
     capacity = pick_lists.shape[2]
     ff = w_gate.shape[1]
     slot_count = max(2, (2 * capacity + n_e - 1) // n_e)
     slot_rows = (slot_count + 15) // 16 * 16
-    n_c = 2
+    n_c = 4
     width = feat // n_c
     padded = n_e * slot_rows
     sent = padded - slot_rows
@@ -318,20 +339,15 @@
     sems = pltpu.SemaphoreType.DMA((2, n_c))
     outs = pl.pallas_call(
         functools.partial(layer_kernel, n_dp, n_e, n_c, slot_rows),
-        out_shape=(
-            jax.ShapeDtypeStruct((tok_rows, feat), BF16),
-            jax.ShapeDtypeStruct((tok_rows, feat), BF16),
-            grad,
-            grad,
-            grad,
-        ),
-        in_specs=[vmem] * 4 + [hbm] * 3,
-        out_specs=(vmem, vmem, hbm, hbm, hbm),
+        out_shape=(pltpu.VMEM((tok_rows, feat), BF16),) * 2 + (pltpu.VMEM((ff, feat), BF16),) * 3,
+        in_specs=[pl.BlockSpec(memory_space=pltpu.HBM)] * 7,
+        out_specs=(vmem,) * 5,
         scratch_shapes=[
             pltpu.VMEM((2 * n_e, capacity), jnp.int32),
             pltpu.VMEM((2 * n_e, capacity), F32),
         ]
-        + [pltpu.VMEM((ff, feat), BF16)] * 6
+        + [pltpu.VMEM((tok_rows, feat), BF16)] * 2
+        + [pltpu.VMEM((ff, feat), BF16)] * 3
         + [
             pltpu.VMEM((2, n_c, sent, width), BF16),
             pltpu.VMEM((2, n_c, padded, width), BF16),
@@ -345,10 +361,10 @@
             pltpu.VMEM((total_rows, ff), F32),
         ]
         + [pltpu.VMEM((total_rows, ff), BF16)] * 3
-        + [pltpu.SemaphoreType.DMA((3,))] * 2
+        + [pltpu.SemaphoreType.DMA((9,))]
         + [sems] * 8,
         compiler_params=pltpu.CompilerParams(
-            collective_id=0, has_side_effects=True, vmem_limit_bytes=56 * 2**20
+            collective_id=0, has_side_effects=True, vmem_limit_bytes=59 * 2**20
         ),
         cost_estimate=pl.CostEstimate(
             flops=18 * total_rows * ff * feat,
@@ -357,7 +373,15 @@
         ),
         name="expert_layer",
     )(tokens, cotangent, pick_lists[0], combine[0], w_gate[0], w_up[0], w_down[0])
-    layer_out, tokens_grad, grad_gate, grad_up, grad_down = outs
+    layer_out, tokens_grad, grad_gate, grad_up, grad_down = pl.pallas_call(
+        store_kernel,
+        out_shape=[jax.ShapeDtypeStruct(o.shape, o.dtype) for o in outs],
+        in_specs=[vmem] * 5,
+        out_specs=[hbm] * 5,
+        scratch_shapes=[pltpu.SemaphoreType.DMA((5,))],
+        compiler_params=pltpu.CompilerParams(vmem_limit_bytes=16 * 2**20),
+        name="store_results",
+    )(*outs)
     return (layer_out, tokens_grad, grad_gate[None], grad_up[None], grad_down[None])
 
 

time: 68.1 us -> 59.2 us (0.87)
  local copies, waits for them, and re-layouts: 7.6 us -> 0 us
  Pallas kernels: 59.6 us -> 58.4 us
    unnamed x11 -> x0, local copies, waits for them, and re-layouts: 7.6 us -> none
    pallas_call x1, Pallas kernels: 59.6 us -> 56.5 us  [per_device(): pl.pallas_call(functools.partial(layer_kernel, n_dp, n_e, n_c, slot_rows)...]
    pallas_call x0 -> x1, Pallas kernels: none -> 1.88 us  [per_device(): pl.pallas_call(store_kernel, out_shape=[jax.ShapeDtypeStruct(o.shape, o.d...]
where the time goes in v2:
time: 59.2 us; the launch traced here: 59 us
  Pallas kernels  58.4 us (99%)
  between operations  0.64 us (1%)
    pallas_call x1, Pallas kernels, per_device(): pl.pallas_call(functools.partial(layer_kernel, n_dp, n_e, n_c, slot_rows)...  56.5 us
    pallas_call x1, Pallas kernels, per_device(): pl.pallas_call(store_kernel, out_shape=[jax.ShapeDtypeStruct(o.shape, o.d...  1.88 us

profile of v2, /device:TPU:0, one launch (start us, length us, event | category | flops | bytes accessed | tf_op | source)
XLA Modules:
  0.0 59.0 jit_solution(2520633582250261539)
XLA Ops:
  0.6 56.5 %expert_layer.1 = (bf16[128,1024]{1,0:T(8,128)(2,1)S(1)}, bf16[128,1024]{1,0:T(8,128)(2,1)S(1)}, bf16[512,1024]{1,0:T(8,128)(2,1)S(1)}, bf16[512,1024]{1,0:T(8,128)(2,1)S(1)}, bf16[512,1024]{1,0:T(8,128)(2,1)S(1)}) custom-call(bf16[128,1024]{1,0:T(8,128)(2,1)} %tok_hbm.1, bf16[128,1024]{1,0:T(8,128)(2,1)} %cot_hbm.1, s32[16,128]{1,0:T(8,128)} %bitcast.14, ...), custom_call_target="tpu_custom_call" | custom-call | flops 2415919104 | bytes 7340032 | tf_op jit(solution)/shard_map/expert_layer/pallas_call | solution.py:340
  57.1 1.9 %store_results.1 = (bf16[128,1024]{1,0:T(8,128)(2,1)}, bf16[128,1024]{1,0:T(8,128)(2,1)}, bf16[512,1024]{1,0:T(8,128)(2,1)}, bf16[512,1024]{1,0:T(8,128)(2,1)}, bf16[512,1024]{1,0:T(8,128)(2,1)}) custom-call(bf16[128,1024]{1,0:T(8,128)(2,1)S(1)} %get-tuple-element.15.refs_0_, bf16[128,1024]{1,0:T(8,128)(2,1)S(1)} %get-tuple-element.16.refs_1_, ...), custom_call_target="tpu_custom_call" | custom-call | tf_op jit(solution)/shard_map/store_results/pallas_call | solution.py:376

commit v3 on v2

--- a/solution.py
+++ b/solution.py
@@ -82,13 +82,10 @@
     comb_t = jnp.concatenate([comb_rel] * copies, axis=0).T
     base = (me * tok_rows).astype(F32)
     token_id = lax.broadcasted_iota(jnp.int32, (1, tok_rows), 1).astype(F32) + base
-    member_rows, weight_rows = [], []
+    member_rows = []
     for k in range(n_e):
         same = list_t[:, k : k + 1] == token_id
         member_rows.append(jnp.sum(jnp.where(same, 1.0, 0.0), axis=0, keepdims=True))
-        weight_rows.append(
-            jnp.sum(jnp.where(same, comb_t[:, k : k + 1], 0.0), axis=0, keepdims=True)
-        )
     member = jnp.concatenate(member_rows, axis=0)
     t_from = lax.broadcasted_iota(jnp.int32, (tok_rows, tok_rows), 0)
     t_to = lax.broadcasted_iota(jnp.int32, (tok_rows, tok_rows), 1)
@@ -98,11 +95,7 @@
     slot_id = lax.broadcasted_iota(jnp.int32, (slot_rows, tok_rows), 0).astype(F32)
     hits = [slot_id == rank[k : k + 1, :] for k in range(n_e)]
     pick = jnp.concatenate([jnp.where(h, 1.0, 0.0) for h in hits], axis=0)
-    pick_w = jnp.concatenate(
-        [jnp.where(h, weight_rows[k], 0.0) for k, h in enumerate(hits)], axis=0
-    )
     pick_b = pick.astype(BF16)
-    row_weight = jnp.sum(pick_w, axis=1, keepdims=True)
 
     def to_experts(a, c):
         def step(i, carry):
@@ -173,6 +166,16 @@
     early[4].wait()
     for c in range(n_c):
         dispatch(0, c)
+    weight_rows = []
+    for k in range(n_e):
+        same = list_t[:, k : k + 1] == token_id
+        weight_rows.append(
+            jnp.sum(jnp.where(same, comb_t[:, k : k + 1], 0.0), axis=0, keepdims=True)
+        )
+    pick_w = jnp.concatenate(
+        [jnp.where(h, weight_rows[k], 0.0) for k, h in enumerate(hits)], axis=0
+    )
+    row_weight = jnp.sum(pick_w, axis=1, keepdims=True)
     early[5].wait()
     for c in range(2):
         dispatch(1, c)

time: 59.2 us -> 59.2 us (level)
  no operation moved by 1% of the time
where the time goes in v3:
time: 59.2 us; the launch traced here: 59 us
  Pallas kernels  58.4 us (99%)
  between operations  0.64 us (1%)
    pallas_call x1, Pallas kernels, per_device(): pl.pallas_call(functools.partial(layer_kernel, n_dp, n_e, n_c, slot_rows)...  56.5 us
    pallas_call x1, Pallas kernels, per_device(): pl.pallas_call(store_kernel, out_shape=[jax.ShapeDtypeStruct(o.shape, o.d...  1.88 us

profile of v3, /device:TPU:0, one launch (start us, length us, event | category | flops | bytes accessed | tf_op | source)
XLA Modules:
  0.0 59.0 jit_solution(9889871441397354189)
XLA Ops:
  0.6 56.5 %expert_layer.1 = (bf16[128,1024]{1,0:T(8,128)(2,1)S(1)}, bf16[128,1024]{1,0:T(8,128)(2,1)S(1)}, bf16[512,1024]{1,0:T(8,128)(2,1)S(1)}, bf16[512,1024]{1,0:T(8,128)(2,1)S(1)}, bf16[512,1024]{1,0:T(8,128)(2,1)S(1)}) custom-call(bf16[128,1024]{1,0:T(8,128)(2,1)} %tok_hbm.1, bf16[128,1024]{1,0:T(8,128)(2,1)} %cot_hbm.1, s32[16,128]{1,0:T(8,128)} %bitcast.14, ...), custom_call_target="tpu_custom_call" | custom-call | flops 2415919104 | bytes 7340032 | tf_op jit(solution)/shard_map/expert_layer/pallas_call | solution.py:343
  57.1 1.9 %store_results.1 = (bf16[128,1024]{1,0:T(8,128)(2,1)}, bf16[128,1024]{1,0:T(8,128)(2,1)}, bf16[512,1024]{1,0:T(8,128)(2,1)}, bf16[512,1024]{1,0:T(8,128)(2,1)}, bf16[512,1024]{1,0:T(8,128)(2,1)}) custom-call(bf16[128,1024]{1,0:T(8,128)(2,1)S(1)} %get-tuple-element.15.refs_0_, bf16[128,1024]{1,0:T(8,128)(2,1)S(1)} %get-tuple-element.16.refs_1_, ...), custom_call_target="tpu_custom_call" | custom-call | tf_op jit(solution)/shard_map/store_results/pallas_call | solution.py:379
